TPU v7x, 256 devices: a whole 4x4x8 slice. The times are simulated.
256 devices in a mesh: sect: 8 (over y, core), dev: 32 (over z, x).
Axes of the slice: x: 4, y: 4, z: 8, core: 2. Of those that a mesh axis runs over, the one named last changes fastest.
Arguments:
- prompt_lengths: int32 [8, 256], P(None, 'dev'), may hold values from 64 to 128, as said below
- owner_map: int32 [8, 256], P(None, 'dev'), may hold values from 0 to 63, as said below
- block_table: int32 [8, 256, 2], P(None, 'dev'), may hold values from 0 to 15, as said below
- pool_blocks: bfloat16 [8, 512, 64, 576], P('sect', 'dev'), may hold values from -4.5 to 4.5
- queries: bfloat16 [4, 2048, 128, 576], P(None, ('sect', 'dev')), may hold values from -48 to 48
- new_latents: bfloat16 [4, 2048, 576], P(None, ('sect', 'dev')), may hold values from -4.5 to 4.5
- value_up: bfloat16 [128, 512, 128], P('dev'), may hold values from -1.5 to 1.5
- out_proj: bfloat16 [16384, 7168], P('dev'), may hold values from -0.046875 to 0.046875
Outputs:
- decoded: bfloat16 [4, 2048, 7168], P(None, ('sect', 'dev'))
Inputs may be any that keep to these rules, and one draw needn't show every extreme that they name: `prompt_lengths`: in each section some request has length 128. Within each device index d, the entries owner_map[p, d * 8 + i] over all p and i name every decode slot 0 to 63 once, and the 8 requests of one section and device index name 8 different sections g. `block_table`: the entries of the 8 requests of one section and device index form a permutation of 0 to 15.
All inputs are finite; a program needn't handle non-finite values.
Results may differ from a plain program's by a relative error of at most 0.02.
Values may be sent and summed in bfloat16 or wider, within the bound.
A program may use at most 128 MiB of HBM per device.

v0:
```python
import jax
import jax.numpy as jnp
from jax import lax
from jax.sharding import PartitionSpec as P

LAT = 512


score_scale = 192.0 ** (-0.5)
masked_score = -1e30


def attend(query_part, key_rows, lengths, step_ids, cached_rows):
    scores = (
        jnp.einsum("rkhw,rtw->rkht", query_part, key_rows, preferred_element_type=jnp.float32)
        * score_scale
    )
    position = jnp.arange(key_rows.shape[1])
    cached_live = position[None, None, :] < lengths[:, None, None]
    fresh_live = position[None, None, :] - cached_rows <= step_ids[None, :, None]
    live_mask = jnp.where(position[None, None, :] < cached_rows, cached_live, fresh_live)
    scores = jnp.where(live_mask[:, :, None, :], scores, masked_score)
    highest = jnp.max(scores, axis=-1, keepdims=True)
    weights = jnp.exp(scores - highest)
    rounded = (weights / jnp.sum(weights, axis=-1, keepdims=True)).astype(jnp.bfloat16)
    latent_rows = key_rows[:, :, :LAT]
    return jnp.einsum(
        "rkht,rtc->rkhc", rounded, latent_rows, preferred_element_type=jnp.float32
    ).astype(jnp.bfloat16)


def project(latent_out, value_up, out_proj):
    values = jnp.einsum(
        "...hc,hcv->...hv", latent_out, value_up, preferred_element_type=jnp.float32
    ).astype(jnp.bfloat16)
    flattened = values.reshape(values.shape[:-2] + (values.shape[-2] * values.shape[-1],))
    return jnp.einsum("...k,kd->...d", flattened, out_proj, preferred_element_type=jnp.float32)


def on_device(
    prompt_lengths, owner_map, block_table, pool_blocks, queries, new_latents, value_up, out_proj
):
    sections = lax.axis_size("sect")
    my_sect = lax.axis_index("sect")
    req_dev = queries.shape[1]
    max_blocks = block_table.shape[2]
    block_rows = pool_blocks.shape[2]
    cache_width = pool_blocks.shape[3]
    cached_rows = max_blocks * block_rows
    slot_ids = jnp.arange(req_dev, dtype=jnp.int32)
    group_ids = jnp.arange(sections, dtype=jnp.int32)
    my_owner = lax.dynamic_index_in_dim(owner_map, my_sect, 0, keepdims=False)
    my_table = lax.dynamic_index_in_dim(block_table, my_sect, 0, keepdims=False)
    heading = (my_owner // req_dev)[None, :] == group_ids[:, None]
    chosen = jnp.sum(jnp.where(heading, slot_ids[None, :], 0), axis=1)
    pool_rows = jnp.take(my_table, chosen, axis=0).reshape(-1)
    packed = jnp.take(pool_blocks[0], pool_rows, axis=0).reshape(
        sections, max_blocks, block_rows, cache_width
    )
    arrived = lax.all_to_all(packed, "sect", split_axis=0, concat_axis=0, tiled=True)
    wanted = my_sect * req_dev + slot_ids
    matches = owner_map[None, :, :] == wanted[:, None, None]
    source = jnp.sum(jnp.where(matches, group_ids[None, :, None], 0), axis=(1, 2))
    lengths = jnp.sum(jnp.where(matches, prompt_lengths[None, :, :], 0), axis=(1, 2))
    caches = jnp.take(arrived, source, axis=0).reshape(req_dev, cached_rows, cache_width)
    key_rows = jnp.concatenate([caches, jnp.transpose(new_latents, (1, 0, 2))], axis=1)
    step_count = queries.shape[0]
    step_ids = jnp.arange(step_count, dtype=jnp.int32)
    outputs = []
    for step_index in range(step_count):
        latent_out = attend(
            queries[step_index][:, None],
            key_rows,
            lengths,
            step_ids[step_index : step_index + 1],
            cached_rows,
        )[:, 0]
        regrouped = lax.all_to_all(latent_out, "dev", split_axis=1, concat_axis=0, tiled=True)
        partial_value = project(regrouped, value_up, out_proj)
        outputs.append(
            lax.psum_scatter(
                partial_value.astype(jnp.bfloat16), "dev", scatter_dimension=0, tiled=True
            )
        )
    decoded = jnp.stack(outputs)
    return decoded


def solution(mesh):
    in_specs = (
        P(None, "dev"),
        P(None, "dev"),
        P(None, "dev", None),
        P("sect", "dev", None, None),
        P(None, ("sect", "dev"), None, None),
        P(None, ("sect", "dev"), None),
        P("dev", None, None),
        P("dev", None),
    )
    out_specs = P(None, ("sect", "dev"), None)
    return jax.shard_map(
        on_device, mesh=mesh, in_specs=in_specs, out_specs=out_specs, check_vma=False
    )
```

profile of v0, /device:TPU:2, one launch (start us, length us, event | category | flops | bytes accessed | tf_op | source)
XLA Modules:
  0.0 993.4 jit_solution(13194537101333985525)
XLA Ops:
  6.5 0.8 fusion.57
  7.3 0.1 select_reduce_fusion
  7.5 0.7 dynamic-slice_bitcast_fusion
  8.2 0.1 copy.43
  8.3 0.6 gather_fusion
  8.8 0.1 compare_and_fusion
  8.9 0.1 select_n.176
  9.0 0.8 gather_fusion.1
  9.8 1.3 broadcast_select_fusion
  11.1 4.6 all-to-all-start
  15.7 0.0 reduce-scatter.5.cloned.1.call-start
  15.7 0.7 fusion.58
  16.4 1.3 fusion.52
  17.8 1.3 fusion.50
  19.0 0.0 copy-done.2
  19.1 0.4 fusion.41
  19.5 0.1 fusion.45
  19.6 14.8 %all-to-all-done = bf16[8,2,64,576]{3,2,1,0:T(8,128)(2,1)S(1)} async-done(((bf16[8,2,64,576]{3,2,1,0:T(8,128)(2,1)}), bf16[8,2,64,576]{3,2,1,0:T(8,128)(2,1)S(1)}, u32[]{:S(2)}, u32[]{:S(2)}) %all-to-all-start) | async-done | bytes 1179680 | tf_op jit(solution)/shard_map/all_to_all | solution.py:60
  34.4 1.8 gather_fusion.2
  36.2 1.5 bitcast_select_fusion
  37.7 1.9 fusion.19
  39.6 0.1 fusion.62
  39.7 1.6 convolution_convert_fusion.7
  41.3 1.8 copy.45
  43.1 0.0 copy-start.4
  43.1 39.4 %all_to_all.77 = bf16[8,128,512]{2,0,1:T(8,128)(2,1)S(1)} all-to-all(bf16[8,128,512]{2,0,1:T(8,128)(2,1)S(1)} %copy.45), channel_id=1, replica_groups=mesh['sect'=8,'dev'=32] {'dev'}, dimensions={1} | all-to-all | bytes 2097152 | tf_op jit(solution)/shard_map/all_to_all | solution.py:78
  82.5 0.5 convolution_convert_fusion.11
  83.0 7.0 convolution_convert_fusion.3
  90.0 0.0 reduce-scatter.5.cloned.1.call-update
  90.0 0.0 reduce-scatter.9.cloned.1.call-start
  90.1 1.9 fusion.15
  92.0 0.1 fusion.60
  92.1 1.5 convolution_convert_fusion.5
  93.6 1.8 copy.51
  95.4 0.0 copy-start.5
  95.4 35.9 %all_to_all.78 = bf16[8,128,512]{2,0,1:T(8,128)(2,1)S(1)} all-to-all(bf16[8,128,512]{2,0,1:T(8,128)(2,1)S(1)} %copy.51), channel_id=1, replica_groups=mesh['sect'=8,'dev'=32] {'dev'}, dimensions={1} | all-to-all | bytes 2097152 | tf_op jit(solution)/shard_map/all_to_all | solution.py:78
  131.3 0.5 convolution_convert_fusion.9
  131.8 7.1 convolution_convert_fusion.1
  138.9 0.0 reduce-scatter.9.cloned.1.call-update
  138.9 0.2 reduce-scatter.7.cloned.1.call-start
  139.1 1.9 fusion.17
  141.0 0.1 fusion.61
  141.2 1.5 convolution_convert_fusion.6
  142.7 1.8 copy.48
  144.5 0.0 copy-start.6
  144.5 36.1 %all_to_all.79 = bf16[8,128,512]{2,0,1:T(8,128)(2,1)S(1)} all-to-all(bf16[8,128,512]{2,0,1:T(8,128)(2,1)S(1)} %copy.48), channel_id=1, replica_groups=mesh['sect'=8,'dev'=32] {'dev'}, dimensions={1} | all-to-all | bytes 2097152 | tf_op jit(solution)/shard_map/all_to_all | solution.py:78
  180.6 0.5 convolution_convert_fusion.10
  181.1 7.2 convolution_convert_fusion.2
  188.3 0.0 reduce-scatter.7.cloned.1.call-update
  188.3 0.0 reduce-scatter.11.cloned.1.call-start
  188.4 1.9 fusion.13
  190.2 0.1 fusion.59
  190.4 1.5 convolution_convert_fusion.4
  191.9 1.8 copy.54
  193.7 0.0 copy-start.7
  193.7 32.6 %all_to_all.80 = bf16[8,128,512]{2,0,1:T(8,128)(2,1)S(1)} all-to-all(bf16[8,128,512]{2,0,1:T(8,128)(2,1)S(1)} %copy.54), channel_id=1, replica_groups=mesh['sect'=8,'dev'=32] {'dev'}, dimensions={1} | all-to-all | bytes 2097152 | tf_op jit(solution)/shard_map/all_to_all | solution.py:78
  226.4 0.5 convolution_convert_fusion.8
  226.9 7.1 convolution_convert_fusion
  234.0 0.0 reduce-scatter.11.cloned.1.call-update
  234.0 84.8 %reduce-scatter.5.cloned.1.call-done = bf16[8,7168]{1,0:T(8,128)(2,1)} async-done(((bf16[256,7168]{1,0:T(8,128)(2,1)}), bf16[8,7168]{1,0:T(8,128)(2,1)}) %reduce-scatter.5.cloned.1.call-update) | async-done | bytes 114704 | tf_op jit(solution)/shard_map/reduce_scatter | solution.py:81
  318.9 222.3 %reduce-scatter.9.cloned.1.call-done = bf16[8,7168]{1,0:T(8,128)(2,1)} async-done(((bf16[256,7168]{1,0:T(8,128)(2,1)}), bf16[8,7168]{1,0:T(8,128)(2,1)}) %reduce-scatter.9.cloned.1.call-update) | async-done | bytes 114704 | tf_op jit(solution)/shard_map/reduce_scatter | solution.py:81
  541.2 221.7 %reduce-scatter.7.cloned.1.call-done = bf16[8,7168]{1,0:T(8,128)(2,1)} async-done(((bf16[256,7168]{1,0:T(8,128)(2,1)}), bf16[8,7168]{1,0:T(8,128)(2,1)}) %reduce-scatter.7.cloned.1.call-update) | async-done | bytes 114704 | tf_op jit(solution)/shard_map/reduce_scatter | solution.py:81
  762.9 222.1 %reduce-scatter.11.cloned.1.call-done = bf16[8,7168]{1,0:T(8,128)(2,1)} async-done(((bf16[256,7168]{1,0:T(8,128)(2,1)}), bf16[8,7168]{1,0:T(8,128)(2,1)}) %reduce-scatter.11.cloned.1.call-update) | async-done | bytes 114704 | tf_op jit(solution)/shard_map/reduce_scatter | solution.py:81
  985.0 1.9 pad_maximum_fusion.2
  (23 shorter events, 0.1 us)
Async XLA Ops:
  6.5 2.5 copy-start
  11.1 6.7 copy-start.1
  11.1 8.0 copy-start.2
  11.1 8.0 copy-start.3
  11.1 23.4 %all-to-all-start = ((bf16[8,2,64,576]{3,2,1,0:T(8,128)(2,1)}), bf16[8,2,64,576]{3,2,1,0:T(8,128)(2,1)S(1)}, u32[]{:S(2)}, u32[]{:S(2)}) async-start(bf16[8,2,64,576]{3,2,1,0:T(8,128)(2,1)} %broadcast_select_fusion), calls=%async_computation | async-start | bytes 2621440 | tf_op jit(solution)/shard_map/all_to_all | solution.py:60
  15.7 303.2 %reduce-scatter.5.cloned.1.call-start = ((), (), s32[]{:S(2)}) async-start(), calls=%async_computation.9 | async-start | bytes 3784704 | tf_op jit(solution)/shard_map/reduce_scatter | solution.py:81
  43.1 39.4 %copy-start.4 = (bf16[4,512,128]{2,1,0:T(8,128)(2,1)S(1)}, bf16[4,512,128]{2,1,0:T(8,128)(2,1)}, u32[]{:S(2)}) copy-start(bf16[4,512,128]{2,1,0:T(8,128)(2,1)} %param.14) | copy-start | bytes 1572868
  90.0 451.2 %reduce-scatter.9.cloned.1.call-start = ((), (), s32[]{:S(2)}) async-start(), calls=%async_computation.11 | async-start | bytes 3784704 | tf_op jit(solution)/shard_map/reduce_scatter | solution.py:81
  95.4 35.9 %copy-start.5 = (bf16[4,512,128]{2,1,0:T(8,128)(2,1)S(1)}, bf16[4,512,128]{2,1,0:T(8,128)(2,1)}, u32[]{:S(2)}) copy-start(bf16[4,512,128]{2,1,0:T(8,128)(2,1)} %param.14) | copy-start | bytes 1572868
  138.9 624.0 %reduce-scatter.7.cloned.1.call-start = ((), (), s32[]{:S(2)}) async-start(), calls=%async_computation.10 | async-start | bytes 3784704 | tf_op jit(solution)/shard_map/reduce_scatter | solution.py:81
  144.5 36.1 %copy-start.6 = (bf16[4,512,128]{2,1,0:T(8,128)(2,1)S(1)}, bf16[4,512,128]{2,1,0:T(8,128)(2,1)}, u32[]{:S(2)}) copy-start(bf16[4,512,128]{2,1,0:T(8,128)(2,1)} %param.14) | copy-start | bytes 1572868
  188.3 796.7 %reduce-scatter.11.cloned.1.call-start = ((), (), s32[]{:S(2)}) async-start(), calls=%async_computation.12 | async-start | bytes 3784704 | tf_op jit(solution)/shard_map/reduce_scatter | solution.py:81
  193.7 32.6 %copy-start.7 = (bf16[4,512,128]{2,1,0:T(8,128)(2,1)S(1)}, bf16[4,512,128]{2,1,0:T(8,128)(2,1)}, u32[]{:S(2)}) copy-start(bf16[4,512,128]{2,1,0:T(8,128)(2,1)} %param.14) | copy-start | bytes 1572868
Sparse Core Ops, SparseCore 0:
  90.2 228.6 reduce-scatter.4
  323.3 217.9 reduce-scatter.8
  545.1 217.7 reduce-scatter.6
  767.1 217.8 reduce-scatter.10
where the time goes:
time: 995 us; the launch traced here: 993 us
  waiting for transfers between devices  766 us (77%)
  blocking collectives  144 us (14%)
  matrix products  44 us (4%)
  between operations  13.4 us (1%)
  local copies, waits for them, and re-layouts  11.9 us (1%)
    reduce_scatter x4, waiting for transfers between devices, on_device(): lax.psum_scatter(partial_value.astype(jnp.bfloat16), 'dev', scatter_dimen...  751 us
    all_to_all x4, blocking collectives, on_device(): lax.all_to_all(latent_out, 'dev', split_axis=1, concat_axis=0, tiled=True)  144 us
    dot_general x4, matrix products, project(): jnp.einsum('...k,kd->...d', flattened, out_proj, preferred_element_type=j...  28.3 us
  transfers between devices with their start and end apart: 5, of which 5 were waited for; matrix products, arithmetic and copies ran while one was open for 4% of the time, Pallas kernels for 0%

commit v1 on v0

v1 whole, which is shorter than its diff:
```python
import jax
import jax.numpy as jnp
from jax import lax
from jax.experimental import pallas as pl
from jax.experimental.pallas import tpu as pltpu
from jax.sharding import PartitionSpec as P

MESH = pl.DeviceIdType.MESH
CHIPS_X = 4
GROUP = 4
score_scale = 192.0 ** (-0.5)
masked_score = -1e30


def ilog2(n):
    return n.bit_length() - 1


def nt_dot(a, b):
    return lax.dot_general(a, b, (((1,), (1,)), ((), ())), preferred_element_type=jnp.float32)


def mm(a, b):
    return jnp.dot(a, b, preferred_element_type=jnp.float32)


def make_kernel(sections, chips_z, chips_x, steps, req, heads, lat_w, width, vdim, model, block):
    Y, Z, X = sections // 2, chips_z, chips_x
    HD = heads // (Z * X)
    HZ = HD * X
    NPG = req // GROUP
    PS = GROUP * steps
    CR = 2 * block
    KR = CR + 128
    NX = model // X
    NT = 256
    KD = HD * vdim
    PV, PW = lat_w // (2 * Y), KD // (2 * Y)

    def kernel(
        owner_ref, table_ref, len_ref, pool_hbm, q_hbm, new_ref, vu_hbm, op_hbm, out_ref,
        pool, q, pk, keys, lat, snd, rcv, vu, val, va, w, po, rs, so, fin,
        lsem, cs, cr, v1s, v1r, v2s, v2r, v3s, v3r, w1s, w1r, w2s, w2r, w3s, w3r,
        ls, lr, zs, zr, gs, gr, ss, sr, fs, fr,
    ):
        sect = lax.axis_index("sect")
        dev = lax.axis_index("dev")
        y, c = sect // 2, sect % 2
        z, x = dev // X, dev % X
        sibling = y * 2 + (1 - c)
        piece = c * Y + y
        sends = []

        def at_sect(r):
            return ((sect + r) % sections, dev)

        def at_y(r):
            return (((y + r) % Y) * 2 + c, dev)

        def at_z(r):
            return (sect, ((z + r) % Z) * X + x)

        def at_x(r):
            return (sect, z * X + (x + r) % X)

        def remote(src, dst, send_sem, recv_sem, to):
            return pltpu.make_async_remote_copy(
                src_ref=src, dst_ref=dst, send_sem=send_sem, recv_sem=recv_sem,
                device_id=to, device_id_type=MESH,
            )

        def send(src, dst, send_sem, recv_sem, to):
            copy = remote(src, dst, send_sem, recv_sem, to)
            copy.start()
            sends.append(copy)

        def arrived(src, dst, send_sem, recv_sem, to):
            remote(src, dst, send_sem, recv_sem, to).wait_recv()

        load_pool = pltpu.make_async_copy(pool_hbm.at[0], pool, lsem.at[0])
        load_q = pltpu.make_async_copy(q_hbm, q, lsem.at[1])
        load_vu = pltpu.make_async_copy(vu_hbm, vu.at[0], lsem.at[2])
        own_cols = pl.ds(pl.multiple_of(x * NX, 128), NX)
        load_w = pltpu.make_async_copy(op_hbm.at[:, own_cols], w.at[0], lsem.at[3])
        load_pool.start()
        load_q.start()
        load_vu.start()
        load_w.start()

        barrier = pltpu.get_barrier_semaphore()
        peers = [at_sect(r) for r in range(1, sections)]
        peers += [at_z(r) for r in range(1, Z)] + [at_x(r) for r in range(1, X)]
        for peer in peers:
            pl.semaphore_signal(barrier, inc=1, device_id=peer, device_id_type=MESH)

        new_rows = new_ref[...].astype(jnp.float32).reshape(steps * req, width)
        new_rows = new_rows.astype(jnp.bfloat16)
        pick_u = lax.broadcasted_iota(jnp.int32, (16, steps * req), 0)
        pick_i = lax.broadcasted_iota(jnp.int32, (16, steps * req), 1)

        def slot_and_length(k):
            source = lax.rem(sect - k + sections, sections)
            slot, length = jnp.int32(0), jnp.int32(0)
            for i in range(req):
                owner = owner_ref[source, i]
                mine = lax.div(owner, req) == sect
                slot += jnp.where(mine, lax.rem(owner, req), 0)
                length += jnp.where(mine, len_ref[source, i], 0)
            return slot, length

        def fresh(k, carry):
            slot, _ = slot_and_length(k)
            pick = (pick_u == (pick_i >> ilog2(req))) & ((pick_i & (req - 1)) == slot)
            rows = mm(pick.astype(jnp.bfloat16), new_rows)
            keys[k, pl.ds(CR, 16), :] = rows.astype(jnp.bfloat16)
            keys[k, pl.ds(CR + 16, KR - CR - 16), :] = jnp.zeros((KR - CR - 16, width), jnp.bfloat16)
            return carry

        lax.fori_loop(0, req, fresh, 0)
        load_pool.wait()

        def pack(r):
            target = lax.rem(sect + r, sections)
            first, second = jnp.int32(0), jnp.int32(0)
            for i in range(req):
                hit = lax.div(owner_ref[sect, i], req) == target
                first += jnp.where(hit, table_ref[sect, i, 0], 0)
                second += jnp.where(hit, table_ref[sect, i, 1], 0)
            return pool[first], pool[second]

        def pack_remote(r, carry):
            a, b = pack(r)
            pk[r, 0:block, :] = a
            pk[r, block:CR, :] = b
            return carry

        lax.fori_loop(1, sections, pack_remote, 0)
        a, b = pack(0)
        keys[0, 0:block, :] = a
        keys[0, block:CR, :] = b

        pl.semaphore_wait(barrier, len(peers))

        def cache_args(r):
            return pk.at[r], keys.at[r, pl.ds(0, CR), :], cs.at[r], cr.at[r], at_sect(r)

        for r in range(1, sections):
            send(*cache_args(r))

        vrows = pl.ds(pl.multiple_of(piece * PV, PV), PV)
        wrows = pl.ds(pl.multiple_of(piece * PW, PW), PW)

        def v1_args(r):
            return vu_hbm.at[:, vrows, :], vu.at[r, :, vrows, :], v1s.at[r], v1r.at[r], at_z(r)

        def w1_args(r):
            cols = pl.ds(pl.multiple_of(((x + r) % X) * NX, 128), NX)
            return op_hbm.at[wrows, cols], w.at[r, wrows, :], w1s.at[r], w1r.at[r], at_x(r)

        def v2_args(r, rows):
            part = vu.at[pl.ds(1, Z - 1), :, rows, :]
            return part, part, v2s.at[r], v2r.at[r], at_y(r)

        def w2_args(r, rows):
            part = w.at[pl.ds(1, X - 1), rows, :]
            return part, part, w2s.at[r], w2r.at[r], at_y(r)

        def v3_args(core):
            rows = pl.ds(pl.multiple_of(core * (lat_w // 2), PV), lat_w // 2)
            part = vu.at[pl.ds(1, Z - 1), :, rows, :]
            return part, part, v3s.at[0], v3r.at[0], (sibling, dev)

        def w3_args(core):
            rows = pl.ds(pl.multiple_of(core * (KD // 2), PW), KD // 2)
            part = w.at[pl.ds(1, X - 1), rows, :]
            return part, part, w3s.at[0], w3r.at[0], (sibling, dev)

        def piece_rows(r, size):
            return pl.ds(pl.multiple_of((c * Y + (y - r + Y) % Y) * size, size), size)

        for r in range(1, Z):
            send(*v1_args(r))
        for r in range(1, X):
            send(*w1_args(r))

        swap_out = lax.broadcasted_iota(jnp.int32, (HZ * PS, HZ * PS), 0)
        swap_in = lax.broadcasted_iota(jnp.int32, (HZ * PS, HZ * PS), 1)
        swap = ((swap_out >> ilog2(PS)) == (swap_in & (HZ - 1))) & (
            (swap_out & (PS - 1)) == (swap_in >> ilog2(HZ))
        )
        swap = swap.astype(jnp.bfloat16)
        load_q.wait()

        def attend(k, k4):
            slot, length = slot_and_length(k)
            q_lat = q[:, slot, :, 0:lat_w].reshape(steps * heads, lat_w)
            q_rope = q[:, slot, :, lat_w:width].reshape(steps * heads, width - lat_w)
            key_lat = keys[k, :, 0:lat_w]
            key_rope = keys[k, :, lat_w:width]
            scores = (nt_dot(q_lat, key_lat) + nt_dot(q_rope, key_rope)) * score_scale
            scores = scores.reshape(steps, heads, KR)
            col = lax.broadcasted_iota(jnp.int32, scores.shape, 2)
            step = lax.broadcasted_iota(jnp.int32, scores.shape, 0)
            held = jnp.where(col < CR, length, CR + 1 + step)
            scores = jnp.where(col < held, scores, masked_score)
            weights = jnp.exp(scores - jnp.max(scores, axis=-1, keepdims=True))
            probs = weights * (1.0 / jnp.sum(weights, axis=-1, keepdims=True))
            probs = probs.astype(jnp.bfloat16).reshape(steps * heads, KR)
            out = mm(probs, key_lat).astype(jnp.bfloat16)
            lat[k4] = out.reshape(steps, heads, lat_w)

        def latent_args(r, pg):
            to = (x + r) % X
            return snd.at[to, pg], rcv.at[x, pg], ls.at[pg, r], lr.at[pg, r], at_x(r)

        def latent_from(r, pg):
            source = (x - r + X) % X
            return snd.at[source, pg], rcv.at[source, pg], ls.at[pg, r], lr.at[pg, r], at_x(r)

        local_latents = []

        def attention(pg):
            def one(k4, carry):
                k = pg * GROUP + k4

                @pl.when(k > 0)
                def _():
                    arrived(pk.at[k], keys.at[k, pl.ds(0, CR), :], cs.at[k], cr.at[k], at_sect(k))

                attend(k, k4)
                return carry

            lax.fori_loop(0, GROUP, one, 0)

            def turn(zz, carry):
                part = lat[:, :, pl.ds(pl.multiple_of(zz * HZ, HZ), HZ), :]
                turned = mm(swap, part.reshape(PS * HZ, lat_w)).astype(jnp.bfloat16)
                snd[:, pg, zz] = turned.reshape(X, HD, PS, lat_w)
                return carry

            lax.fori_loop(0, Z, turn, 0)
            for r in range(1, X):
                send(*latent_args(r, pg))
            own = pltpu.make_async_copy(snd.at[x, pg], rcv.at[x, pg], lsem.at[4 + pg])
            own.start()
            local_latents.append(own)

        def value_args(r, pg):
            to = (z + r) % Z
            return val.at[to, pg], va.at[0, pg, z], zs.at[pg, r], zr.at[pg, r], at_z(r)

        def value_from(r, pg):
            source = (z - r + Z) % Z
            return val.at[source, pg], va.at[0, pg, source], zs.at[pg, r], zr.at[pg, r], at_z(r)

        local_values = []

        def values(pg):
            for r in range(1, X):
                arrived(*latent_from(r, pg))
            local_latents[pg].wait()

            def ring(r, carry):
                zz = lax.rem(z - r + Z, Z)
                for hh in range(HD):
                    rows = rcv[:, pg, zz, hh].reshape(X * PS, lat_w)
                    part = mm(rows, vu[r, hh]).astype(jnp.bfloat16)
                    val[zz, pg, :, hh * vdim : (hh + 1) * vdim] = part
                return carry

            lax.fori_loop(0, Z, ring, 0)
            for r in range(1, Z):
                send(*value_args(r, pg))
            own = pltpu.make_async_copy(val.at[z, pg], va.at[0, pg, z], lsem.at[4 + NPG + pg])
            own.start()
            local_values.append(own)

        def gather_args(r, pg):
            return va.at[0, pg], va.at[r, pg], gs.at[pg, r], gr.at[pg, r], at_x(r)

        def gather_start(pg):
            for r in range(1, Z):
                arrived(*value_from(r, pg))
            local_values[pg].wait()
            for r in range(1, X):
                send(*gather_args(r, pg))

        def sum_args(r, pg):
            to = (z + r) % Z
            return po.at[to, pg], rs.at[r, pg], ss.at[pg, r], sr.at[pg, r], at_z(r)

        def project(pg):
            for r in range(1, X):
                arrived(*gather_args(r, pg))

            def tile(n, carry):
                cols = pl.ds(pl.multiple_of(n * NT, NT), NT)
                acc = mm(va[0, pg].reshape(Z * X * PS, KD), w[0, :, cols])
                for r in range(1, X):
                    acc += mm(va[r, pg].reshape(Z * X * PS, KD), w[r, :, cols])
                po[:, pg, :, cols] = acc.astype(jnp.bfloat16).reshape(Z, X * PS, NT)
                return carry

            lax.fori_loop(0, NX // NT, tile, 0)
            for r in range(1, Z):
                send(*sum_args(r, pg))

        def final_args(r, pg):
            to = (x + r) % X
            return so.at[pg, to], fin.at[x, pg], fs.at[pg, r], fr.at[pg, r], at_x(r)

        def final_from(r, pg):
            source = (x - r + X) % X
            return so.at[pg, source], fin.at[source, pg], fs.at[pg, r], fr.at[pg, r], at_x(r)

        local_final = []

        def reduce(pg):
            for r in range(1, Z):
                arrived(*sum_args(r, pg))

            def rows_of(xx, carry):
                rows = pl.ds(pl.multiple_of(xx * PS, PS), PS)
                total = po[z, pg, rows, :].astype(jnp.float32)
                for r in range(1, Z):
                    total += rs[r, pg, rows, :].astype(jnp.float32)
                so[pg, xx] = total.astype(jnp.bfloat16)
                return carry

            lax.fori_loop(0, X, rows_of, 0)
            for r in range(1, X):
                send(*final_args(r, pg))
            own = pltpu.make_async_copy(so.at[pg, x], fin.at[x, pg], lsem.at[4 + 2 * NPG + pg])
            own.start()
            local_final.append(own)

        for r in range(1, Z):
            arrived(*v1_args(r))
        for r in range(1, Y):
            send(*v2_args(r, vrows))
        attention(0)
        for r in range(1, X):
            arrived(*w1_args(r))
        for r in range(1, Y):
            send(*w2_args(r, wrows))
        for pg in range(1, NPG):
            attention(pg)
        load_vu.wait()
        for r in range(1, Y):
            arrived(*v2_args(r, piece_rows(r, PV)))
        send(*v3_args(c))
        arrived(*v3_args(1 - c))
        for pg in range(NPG):
            values(pg)
            gather_start(pg)
        load_w.wait()
        for r in range(1, Y):
            arrived(*w2_args(r, piece_rows(r, PW)))
        send(*w3_args(c))
        arrived(*w3_args(1 - c))
        for pg in range(NPG):
            project(pg)
        for pg in range(NPG):
            reduce(pg)

        place_out = lax.broadcasted_iota(jnp.int32, (steps * req, steps * req), 0)
        place_in = lax.broadcasted_iota(jnp.int32, (steps * req, steps * req), 1)
        slots = jnp.zeros((steps * req, steps * req), jnp.int32)
        for k in range(req):
            slot, _ = slot_and_length(k)
            slots = jnp.where((place_in >> ilog2(steps)) == k, slot, slots)
        place = ((place_out >> ilog2(req)) == (place_in & (steps - 1))) & (
            (place_out & (req - 1)) == slots
        )
        place = place.astype(jnp.bfloat16)
        for pg in range(NPG):
            for r in range(1, X):
                arrived(*final_from(r, pg))
            local_final[pg].wait()
        for xs in range(X):
            rows = mm(place, fin[xs].reshape(NPG * PS, NX))
            for s in range(steps):
                part = rows[s * req : (s + 1) * req].astype(jnp.bfloat16)
                out_ref[s, :, xs * NX : (xs + 1) * NX] = part

        for copy in sends:
            copy.wait_send()

    bf = jnp.bfloat16
    dma = pltpu.SemaphoreType.DMA
    scratch = [
        pltpu.VMEM((2 * req, block, width), bf),
        pltpu.VMEM((steps, req, heads, width), bf),
        pltpu.VMEM((sections, CR, width), bf),
        pltpu.VMEM((req, KR, width), bf),
        pltpu.VMEM((GROUP, steps, heads, lat_w), bf),
        pltpu.VMEM((X, NPG, Z, HD, PS, lat_w), bf),
        pltpu.VMEM((X, NPG, Z, HD, PS, lat_w), bf),
        pltpu.VMEM((Z, HD, lat_w, vdim), bf),
        pltpu.VMEM((Z, NPG, X * PS, KD), bf),
        pltpu.VMEM((X, NPG, Z, X * PS, KD), bf),
        pltpu.VMEM((X, KD, NX), bf),
        pltpu.VMEM((Z, NPG, X * PS, NX), bf),
        pltpu.VMEM((Z, NPG, X * PS, NX), bf),
        pltpu.VMEM((NPG, X, PS, NX), bf),
        pltpu.VMEM((X, NPG, PS, NX), bf),
        dma((4 + 3 * NPG,)),
        dma((sections,)), dma((sections,)),
        dma((Z,)), dma((Z,)), dma((Y,)), dma((Y,)), dma((1,)), dma((1,)),
        dma((X,)), dma((X,)), dma((Y,)), dma((Y,)), dma((1,)), dma((1,)),
        dma((NPG, X)), dma((NPG, X)), dma((NPG, Z)), dma((NPG, Z)),
        dma((NPG, X)), dma((NPG, X)), dma((NPG, Z)), dma((NPG, Z)),
        dma((NPG, X)), dma((NPG, X)),
    ]
    return kernel, scratch


def on_device(
    prompt_lengths, owner_map, block_table, pool_blocks, queries, new_latents, value_up, out_proj
):
    sections, devices = lax.axis_size("sect"), lax.axis_size("dev")
    steps, req, heads, width = queries.shape
    _, lat_w, vdim = value_up.shape
    model = out_proj.shape[1]
    block = pool_blocks.shape[2]
    kernel, scratch = make_kernel(
        sections, devices // CHIPS_X, CHIPS_X, steps, req, heads, lat_w, width, vdim, model, block
    )
    smem = pl.BlockSpec(memory_space=pltpu.SMEM)
    vmem = pl.BlockSpec(memory_space=pltpu.VMEM)
    hbm = pl.BlockSpec(memory_space=pl.ANY)
    return pl.pallas_call(
        kernel,
        out_shape=jax.ShapeDtypeStruct((steps, req, model), jnp.bfloat16),
        in_specs=[smem, smem, smem, hbm, hbm, vmem, hbm, hbm],
        out_specs=vmem,
        scratch_shapes=scratch,
        compiler_params=pltpu.CompilerParams(
            collective_id=0, has_side_effects=True, vmem_limit_bytes=60 * 1024 * 1024
        ),
    )(owner_map, block_table, prompt_lengths, pool_blocks, queries, new_latents, value_up, out_proj)


def solution(mesh):
    in_specs = (
        P(None, "dev"),
        P(None, "dev"),
        P(None, "dev", None),
        P("sect", "dev", None, None),
        P(None, ("sect", "dev"), None, None),
        P(None, ("sect", "dev"), None),
        P("dev", None, None),
        P("dev", None),
    )
    out_specs = P(None, ("sect", "dev"), None)
    return jax.shard_map(
        on_device, mesh=mesh, in_specs=in_specs, out_specs=out_specs, check_vma=False
    )
```

time: 995 us -> 204 us (0.21)
  waiting for transfers between devices: 766 us -> 0 us
  Pallas kernels: 0 us -> 189 us
  blocking collectives: 144 us -> 0 us
  matrix products: 44 us -> 0 us
  between operations: 13.4 us -> 0.01 us
    reduce_scatter x4 -> x0, waiting for transfers between devices: 751 us -> none  [on_device(): lax.psum_scatter(partial_value.astype(jnp.bfloat16), 'dev', scatter_dimen...]
    pallas_call x0 -> x1, Pallas kernels: none -> 189 us  [on_device(): pl.pallas_call(kernel, out_shape=jax.ShapeDtypeStruct((steps, req, model)...]
    all_to_all x4 -> x0, blocking collectives: 144 us -> none  [on_device(): lax.all_to_all(latent_out, 'dev', split_axis=1, concat_axis=0, tiled=True)]
    dot_general x16 -> x0, matrix products: 44 us -> none  [the longest x4 28.3 us: project(): jnp.einsum('...k,kd->...d', flattened, out_proj, preferred_element_type=j...]
    all_to_all x1 -> x0, waiting for transfers between devices: 14.8 us -> none  [on_device(): lax.all_to_all(packed, 'sect', split_axis=0, concat_axis=0, tiled=True)]
    unnamed x17 -> x3, local copies, waits for them, and re-layouts: 0.06 us -> 10.9 us
  transfers between devices with their start and end apart: 5 -> 0, of which waited for: 5 -> 0; matrix products, arithmetic and copies ran while one was open for 4% -> 0% of each run, Pallas kernels for 0% -> 0%
where the time goes in v1:
time: 204 us; the launch traced here: 200 us
  Pallas kernels  189 us (93%)
  local copies, waits for them, and re-layouts  10.9 us (5%)
    pallas_call x1, Pallas kernels, on_device(): pl.pallas_call(kernel, out_shape=jax.ShapeDtypeStruct((steps, req, model)...  189 us
    unnamed x3, local copies, waits for them, and re-layouts  10.9 us

profile of v1, /device:TPU:2, one launch (start us, length us, event | category | flops | bytes accessed | tf_op | source)
XLA Modules:
  0.0 200.0 jit_solution(17027426074422170124)
XLA Ops:
  0.0 1.4 copy.9.table_ref
  1.4 7.7 %copy.10.q_hbm = bf16[4,8,128,576]{3,2,1,0:T(8,128)(2,1)} copy(bf16[4,8,128,576]{2,3,1,0:T(8,128)(2,1)} %param.12) | data formatting | bytes 9437184 | tf_op args[4]
  9.1 189.0 %shard_map.82 = bf16[4,8,7168]{2,1,0:T(8,128)(2,1)} custom-call(s32[8,8]{1,0:T(8,128)} %owner_ref.1, s32[8,8,2]{2,1,0:T(8,128)} %copy.9.table_ref, s32[8,8]{1,0:T(8,128)} %len_ref.1, bf16[1,16,64,576]{3,2,1,0:T(8,128)(2,1)} %pool_hbm.1, bf16[4,8,128,576]{3,2,1,0:T(8,128)(2,1)} %copy.10.q_hbm, bf16[4,8,576]{2,1,0:T(8,128)(2,1)} %new_ref.1, ...), custom_call_target="tpu_custom_call" | custom-call | tf_op jit(solution)/shard_map/pallas_call | solution.py:432
  198.1 1.8 copy.12
